TPU v7x, 32 devices: a whole 2x2x4 slice. The times are simulated.
32 devices in a mesh: ctx: 4 (over z), chan: 8 (over y, x, core).
Axes of the slice: x: 2, y: 2, z: 4, core: 2. Of those that a mesh axis runs over, the one named last changes fastest.
Arguments:
- value: bfloat16 [64, 16384], P('chan', 'ctx'), may hold values from -6 to 6
- gate: bfloat16 [64, 16384], P('chan', 'ctx'), may hold values from -6 to 6
- residual: float32 [64, 16384], P('chan', 'ctx'), may hold values from -24 to 24
- rates: float32 [64, 16], P('chan'), may hold values from 3.0517578e-05 to 0.05
- residues: float32 [64, 16], P('chan'), may hold values from -1.5 to 1.5
- skip: float32 [64], P('chan'), may hold values from -3 to 3
- gain: float32 [64], P('chan'), may hold values from 0.5 to 1.5
Outputs:
- mixed: float32 [64, 16384], P('chan', 'ctx')
- normed: bfloat16 [64, 16384], P('chan', 'ctx')
All inputs are finite; a program needn't handle non-finite values.
Results may differ from a plain program's by a relative error of at most 0.0004.
Values may be sent and summed in bfloat16 or wider, within the bound.
A program may use at most 128 MiB of HBM per device.

v0:
```python
import functools

import jax
import jax.numpy as jnp
from jax import lax
from jax.experimental import pallas as pl
from jax.experimental.pallas import tpu as pltpu
from jax.sharding import PartitionSpec as P

CHUNK = 128
F32 = jnp.float32
BF16 = jnp.bfloat16
MESH = pl.DeviceIdType.MESH


def two_terms(x):
    high = x.astype(BF16)
    return high, (x - high.astype(F32)).astype(BF16)


def stack_chunks(x, count):
    return jnp.concatenate([x[:, k * CHUNK:(k + 1) * CHUNK] for k in range(count)], axis=0)


def column_of(ref, count):
    row = lax.broadcasted_iota(jnp.int32, (count, CHUNK), 0)
    out = jnp.zeros((count, CHUNK), F32)
    for c in range(count):
        out = jnp.where(row == c, ref[c], out)
    return out


def kernel(
    n_ctx, n_chan,
    value_ref, gate_ref, residual_ref, rates_ref, residues_ref, skip_ref, gain_ref,
    mixed_ref, normed_ref,
    state_out, state_in, square_out, square_in,
    state_send, state_recv, square_send, square_recv,
):
    ctx = lax.axis_index("ctx")
    chan = lax.axis_index("chan")
    channels, local_len = value_ref.shape
    modes = rates_ref.shape[1]
    lanes = channels * modes
    count = local_len // CHUNK

    barrier = pltpu.get_barrier_semaphore()
    for step in range(1, n_ctx):
        pl.semaphore_signal(
            barrier, inc=1, device_id={"ctx": lax.rem(ctx + step, n_ctx)}, device_id_type=MESH
        )
    for step in range(1, n_chan):
        pl.semaphore_signal(
            barrier, inc=1, device_id={"chan": lax.rem(chan + step, n_chan)}, device_id_type=MESH
        )

    rates = rates_ref[...]
    weights = residues_ref[...] * jnp.sqrt(2.0 * rates)
    row8 = lax.broadcasted_iota(jnp.int32, (channels, lanes), 0)
    lane8 = lax.broadcasted_iota(jnp.int32, (channels, lanes), 1)
    token = lax.broadcasted_iota(jnp.int32, (channels, CHUNK), 1)
    time = token.astype(F32)
    taps = jnp.zeros((channels, CHUNK), F32)
    rate_rows = jnp.zeros((channels, lanes), F32)
    weight_rows = jnp.zeros((channels, lanes), F32)
    for m in range(modes):
        rate = jnp.broadcast_to(rates[:, m:m + 1], (channels, CHUNK))
        weight = jnp.broadcast_to(weights[:, m:m + 1], (channels, CHUNK))
        taps = taps + weight * jnp.exp(-rate * time)
        here = lane8 % modes == m
        rate_rows = jnp.where(here, rate, rate_rows)
        weight_rows = jnp.where(here, weight, weight_rows)
    own = row8 == lane8 // modes
    rate_lane = jnp.sum(jnp.where(own, rate_rows, 0.0), axis=0, keepdims=True)
    weight_lane = jnp.sum(jnp.where(own, weight_rows, 0.0), axis=0, keepdims=True)

    signal = stack_chunks(value_ref[...].astype(F32), count)
    signal16 = signal.astype(BF16)
    place = lax.broadcasted_iota(jnp.int32, (CHUNK, lanes), 0).astype(F32)
    enter = jnp.exp(-rate_lane * (CHUNK - 1.0 - place))
    enter2 = jnp.concatenate(two_terms(enter), axis=1)
    added = jnp.dot(signal16, enter2, preferred_element_type=F32)
    added = added[:, :lanes] + added[:, lanes:]
    chunk_decay = jnp.exp(-rate_lane * float(CHUNK))
    state = jnp.zeros((channels, lanes), F32)
    states = []
    for k in range(count):
        states.append(state)
        chunk = jnp.where(own, added[k * channels:(k + 1) * channels], 0.0)
        state = chunk_decay * state + chunk
    state_out[...] = state

    pl.semaphore_wait(barrier, n_ctx - 1 + n_chan - 1)
    state_copies = []
    for step in range(1, n_ctx):
        copy = pltpu.make_async_remote_copy(
            src_ref=state_out,
            dst_ref=state_in.at[step - 1],
            send_sem=state_send.at[step - 1],
            recv_sem=state_recv.at[step - 1],
            device_id={"ctx": lax.rem(ctx + step, n_ctx)},
            device_id_type=MESH,
        )
        copy.start()
        state_copies.append(copy)

    taps = taps + jnp.where(token == 0, column_of(skip_ref, channels), 0.0)
    target = lax.broadcasted_iota(jnp.int32, (CHUNK, CHUNK), 1)
    source = lax.broadcasted_iota(jnp.int32, (CHUNK, CHUNK), 0)
    channel_of = lax.broadcasted_iota(jnp.int32, (count * channels, CHUNK), 0) % channels
    left, right = [], []
    for c in range(channels):
        wide = jnp.broadcast_to(taps[c:c + 1], (CHUNK, CHUNK))
        turned = pltpu.roll(wide, 0, 1, stride=1, stride_axis=0)
        toeplitz = jnp.where(target >= source, turned, 0.0)
        right.append(jnp.concatenate(two_terms(toeplitz), axis=1))
        left.append(jnp.where(channel_of == c, signal, 0.0).astype(BF16))
    near = jnp.dot(
        jnp.concatenate(left, axis=1), jnp.concatenate(right, axis=0), preferred_element_type=F32
    )
    leave = weight_lane * jnp.exp(-rate_lane * (place + 1.0))
    leave2 = jnp.concatenate(two_terms(leave), axis=0)
    leave2 = jnp.concatenate([leave2, leave2], axis=1)
    power = jnp.exp(
        -rate_lane * (float(CHUNK) * lax.broadcasted_iota(jnp.int32, (count, lanes), 0).astype(F32))
    )

    carry = jnp.zeros((channels, lanes), F32)
    for step in range(1, n_ctx):
        state_copies[step - 1].wait()
        decay = jnp.exp(-rate_lane * float(local_len * (step - 1)))
        carry = carry + jnp.where(ctx >= step, decay, 0.0) * state_in[step - 1]
    full = jnp.concatenate([states[k] + power[k:k + 1] * carry for k in range(count)], axis=0)
    far = lax.dot_general(
        jnp.concatenate(two_terms(full), axis=1), leave2, (((1,), (1,)), ((), ())),
        preferred_element_type=F32,
    )
    both = near + far
    conv = both[:, :CHUNK] + both[:, CHUNK:]
    mixed = stack_chunks(residual_ref[...], count) + stack_chunks(gate_ref[...].astype(F32), count) * conv
    square_out[...] = jnp.sum((mixed * mixed).reshape(count, channels, CHUNK), axis=1)

    square_copies = []
    for step in range(1, n_chan):
        copy = pltpu.make_async_remote_copy(
            src_ref=square_out,
            dst_ref=square_in.at[step - 1],
            send_sem=square_send.at[step - 1],
            recv_sem=square_recv.at[step - 1],
            device_id={"chan": lax.rem(chan + step, n_chan)},
            device_id_type=MESH,
        )
        copy.start()
        square_copies.append(copy)
    gain = column_of(gain_ref, channels)
    for k in range(count):
        mixed_ref[:, k * CHUNK:(k + 1) * CHUNK] = mixed[k * channels:(k + 1) * channels]
    total = square_out[...]
    for step in range(1, n_chan):
        square_copies[step - 1].wait()
        total = total + square_in[step - 1]
    scale = lax.rsqrt(total / float(channels * n_chan) + 1e-06)
    for k in range(count):
        normed = mixed[k * channels:(k + 1) * channels] * scale[k:k + 1] * gain
        normed_ref[:, k * CHUNK:(k + 1) * CHUNK] = normed.astype(BF16)


def local(n_ctx, n_chan, value, gate, residual, rates, residues, skip, gain):
    channels, local_len = value.shape
    lanes = channels * rates.shape[1]
    count = local_len // CHUNK
    vmem = pl.BlockSpec(memory_space=pltpu.VMEM)
    smem = pl.BlockSpec(memory_space=pltpu.SMEM)
    return pl.pallas_call(
        functools.partial(kernel, n_ctx, n_chan),
        out_shape=(
            jax.ShapeDtypeStruct((channels, local_len), F32),
            jax.ShapeDtypeStruct((channels, local_len), BF16),
        ),
        in_specs=[vmem] * 5 + [smem] * 2,
        out_specs=(vmem, vmem),
        scratch_shapes=[
            pltpu.VMEM((channels, lanes), F32),
            pltpu.VMEM((n_ctx - 1, channels, lanes), F32),
            pltpu.VMEM((count, CHUNK), F32),
            pltpu.VMEM((n_chan - 1, count, CHUNK), F32),
            pltpu.SemaphoreType.DMA((n_ctx - 1,)),
            pltpu.SemaphoreType.DMA((n_ctx - 1,)),
            pltpu.SemaphoreType.DMA((n_chan - 1,)),
            pltpu.SemaphoreType.DMA((n_chan - 1,)),
        ],
        compiler_params=pltpu.CompilerParams(
            collective_id=0, has_side_effects=True, vmem_limit_bytes=32 * 1024 * 1024
        ),
        cost_estimate=pl.CostEstimate(
            flops=2 * count * channels * CHUNK * 2 * (channels * CHUNK + 3 * lanes),
            bytes_accessed=14 * channels * local_len,
            transcendentals=64 * 1024,
        ),
    )(value, gate, residual, rates, residues, skip, gain)


def solution(mesh):
    return jax.shard_map(
        functools.partial(local, mesh.shape["ctx"], mesh.shape["chan"]),
        mesh=mesh,
        in_specs=(
            P("chan", "ctx"),
            P("chan", "ctx"),
            P("chan", "ctx"),
            P("chan", None),
            P("chan", None),
            P("chan"),
            P("chan"),
        ),
        out_specs=(P("chan", "ctx"), P("chan", "ctx")),
        check_vma=False,
    )
```

profile of v0, /device:TPU:0, one launch (start us, length us, event | category | flops | bytes accessed | tf_op | source)
XLA Modules:
  0.0 20.1 jit_solution(2992297594869106431)
XLA Ops:
  0.6 0.0 copy-start
  0.6 0.9 %copy-done = f32[8,4096]{1,0:T(8,128)S(1)} copy-done((f32[8,4096]{1,0:T(8,128)S(1)}, f32[8,4096]{1,0:T(8,128)}, u32[]{:S(2)}) %copy-start) | copy-done | bytes 131096
  1.5 0.0 copy-start.1
  1.5 0.8 %copy-done.1 = bf16[8,4096]{1,0:T(8,128)(2,1)S(1)} copy-done((bf16[8,4096]{1,0:T(8,128)(2,1)S(1)}, bf16[8,4096]{1,0:T(8,128)(2,1)}, u32[]{:S(2)}) %copy-start.1) | copy-done | bytes 65560
  2.4 0.0 copy-start.2
  2.4 0.8 %copy-done.2 = bf16[8,4096]{1,0:T(8,128)(2,1)S(1)} copy-done((bf16[8,4096]{1,0:T(8,128)(2,1)S(1)}, bf16[8,4096]{1,0:T(8,128)(2,1)}, u32[]{:S(2)}) %copy-start.2) | copy-done | bytes 65560
  3.2 0.0 copy-start.3
  3.2 0.7 %copy-done.3 = f32[8,16]{1,0:T(8,128)S(1)} copy-done((f32[8,16]{1,0:T(8,128)S(1)}, f32[8,16]{1,0:T(8,128)}, u32[]{:S(2)}) %copy-start.3) | copy-done | bytes 536
  3.9 0.0 copy-start.4
  3.9 0.7 %copy-done.4 = f32[8,16]{1,0:T(8,128)S(1)} copy-done((f32[8,16]{1,0:T(8,128)S(1)}, f32[8,16]{1,0:T(8,128)}, u32[]{:S(2)}) %copy-start.4) | copy-done | bytes 536
  4.6 0.0 copy-start.5
  4.6 0.7 %copy-done.5 = f32[8]{0:T(128)S(1)} copy-done((f32[8]{0:T(128)S(1)}, f32[8]{0:T(128)}, u32[]{:S(2)}) %copy-start.5) | copy-done | bytes 56
  5.2 0.0 copy-start.6
  5.2 0.7 %copy-done.6 = f32[8]{0:T(128)S(1)} copy-done((f32[8]{0:T(128)S(1)}, f32[8]{0:T(128)}, u32[]{:S(2)}) %copy-start.6) | copy-done | bytes 56
  5.9 12.9 %shard_map.86 = (f32[8,4096]{1,0:T(8,128)S(1)}, bf16[8,4096]{1,0:T(8,128)(2,1)S(1)}) custom-call(bf16[8,4096]{1,0:T(8,128)(2,1)S(1)} %copy-done.1, bf16[8,4096]{1,0:T(8,128)(2,1)S(1)} %copy-done.2, f32[8,4096]{1,0:T(8,128)S(1)} %copy-done, f32[8,16]{1,0:T(8,128)S(1)} %copy-done.3, f32[8,16]{1,0:T(8,128)S(1)} %copy-done.4, f32[8]{0:T(128)S(1)} %copy-done.5, ...), custom_call_target="tpu_custom_call" | custom-call | flops 184549376 | bytes 458752 | tf_op jit(solution)/shard_map/pallas_call | solution.py:174
  18.8 0.7 %copy.11 = f32[8,4096]{1,0:T(8,128)} copy(f32[8,4096]{1,0:T(8,128)S(1)} %get-tuple-element.4) | data formatting | bytes 262144
  19.5 0.6 %copy.12 = bf16[8,4096]{1,0:T(8,128)(2,1)} copy(bf16[8,4096]{1,0:T(8,128)(2,1)S(1)} %get-tuple-element.5) | data formatting | bytes 131072
Async XLA Ops:
  0.6 0.9 %copy-start = (f32[8,4096]{1,0:T(8,128)S(1)}, f32[8,4096]{1,0:T(8,128)}, u32[]{:S(2)}) copy-start(f32[8,4096]{1,0:T(8,128)} %residual_ref.1) | copy-start | bytes 393220
  1.5 0.8 %copy-start.1 = (bf16[8,4096]{1,0:T(8,128)(2,1)S(1)}, bf16[8,4096]{1,0:T(8,128)(2,1)}, u32[]{:S(2)}) copy-start(bf16[8,4096]{1,0:T(8,128)(2,1)} %value_ref.1) | copy-start | bytes 196612
  2.4 0.8 %copy-start.2 = (bf16[8,4096]{1,0:T(8,128)(2,1)S(1)}, bf16[8,4096]{1,0:T(8,128)(2,1)}, u32[]{:S(2)}) copy-start(bf16[8,4096]{1,0:T(8,128)(2,1)} %gate_ref.1) | copy-start | bytes 196612
  3.2 0.7 %copy-start.3 = (f32[8,16]{1,0:T(8,128)S(1)}, f32[8,16]{1,0:T(8,128)}, u32[]{:S(2)}) copy-start(f32[8,16]{1,0:T(8,128)} %rates_ref.1) | copy-start | bytes 1540
  3.9 0.7 %copy-start.4 = (f32[8,16]{1,0:T(8,128)S(1)}, f32[8,16]{1,0:T(8,128)}, u32[]{:S(2)}) copy-start(f32[8,16]{1,0:T(8,128)} %residues_ref.1) | copy-start | bytes 1540
  4.6 0.7 %copy-start.5 = (f32[8]{0:T(128)S(1)}, f32[8]{0:T(128)}, u32[]{:S(2)}) copy-start(f32[8]{0:T(128)} %skip_ref.1) | copy-start | bytes 100
  5.2 0.7 %copy-start.6 = (f32[8]{0:T(128)S(1)}, f32[8]{0:T(128)}, u32[]{:S(2)}) copy-start(f32[8]{0:T(128)} %gain_ref.1) | copy-start | bytes 100
where the time goes:
time: 20.4 us; the launch traced here: 20.1 us
  Pallas kernels  12.9 us (63%)
  local copies, waits for them, and re-layouts  6.54 us (32%)
  between operations  0.66 us (3%)
    pallas_call x1, Pallas kernels, local(): pl.pallas_call(functools.partial(kernel, n_ctx, n_chan), out_shape=(jax.S...  12.9 us
    unnamed x16, local copies, waits for them, and re-layouts  6.54 us

commit v1 on v0

--- a/solution.py
+++ b/solution.py
@@ -32,11 +32,24 @@
 
 def kernel(
     n_ctx, n_chan,
-    value_ref, gate_ref, residual_ref, rates_ref, residues_ref, skip_ref, gain_ref,
+    value_hbm, gate_hbm, residual_hbm, rates_hbm, residues_hbm, skip_hbm, gain_hbm,
     mixed_ref, normed_ref,
+    rates_ref, residues_ref, value_ref, skip_ref, residual_ref, gate_ref, gain_ref, load_sem,
     state_out, state_in, square_out, square_in,
     state_send, state_recv, square_send, square_recv,
 ):
+    loads = {}
+    for order, (name, source, target) in enumerate([
+        ("rates", rates_hbm, rates_ref),
+        ("residues", residues_hbm, residues_ref),
+        ("value", value_hbm, value_ref),
+        ("skip", skip_hbm, skip_ref),
+        ("residual", residual_hbm, residual_ref),
+        ("gate", gate_hbm, gate_ref),
+        ("gain", gain_hbm, gain_ref),
+    ]):
+        loads[name] = pltpu.make_async_copy(source, target, load_sem.at[order])
+        loads[name].start()
     ctx = lax.axis_index("ctx")
     chan = lax.axis_index("chan")
     channels, local_len = value_ref.shape
@@ -54,6 +67,8 @@
             barrier, inc=1, device_id={"chan": lax.rem(chan + step, n_chan)}, device_id_type=MESH
         )
 
+    loads["rates"].wait()
+    loads["residues"].wait()
     rates = rates_ref[...]
     weights = residues_ref[...] * jnp.sqrt(2.0 * rates)
     row8 = lax.broadcasted_iota(jnp.int32, (channels, lanes), 0)
@@ -74,6 +89,7 @@
     rate_lane = jnp.sum(jnp.where(own, rate_rows, 0.0), axis=0, keepdims=True)
     weight_lane = jnp.sum(jnp.where(own, weight_rows, 0.0), axis=0, keepdims=True)
 
+    loads["value"].wait()
     signal = stack_chunks(value_ref[...].astype(F32), count)
     signal16 = signal.astype(BF16)
     place = lax.broadcasted_iota(jnp.int32, (CHUNK, lanes), 0).astype(F32)
@@ -104,6 +120,7 @@
         copy.start()
         state_copies.append(copy)
 
+    loads["skip"].wait()
     taps = taps + jnp.where(token == 0, column_of(skip_ref, channels), 0.0)
     target = lax.broadcasted_iota(jnp.int32, (CHUNK, CHUNK), 1)
     source = lax.broadcasted_iota(jnp.int32, (CHUNK, CHUNK), 0)
@@ -125,6 +142,9 @@
         -rate_lane * (float(CHUNK) * lax.broadcasted_iota(jnp.int32, (count, lanes), 0).astype(F32))
     )
 
+    for name in ("residual", "gate", "gain"):
+        loads[name].wait()
+
     carry = jnp.zeros((channels, lanes), F32)
     for step in range(1, n_ctx):
         state_copies[step - 1].wait()
@@ -170,16 +190,24 @@
     lanes = channels * rates.shape[1]
     count = local_len // CHUNK
     vmem = pl.BlockSpec(memory_space=pltpu.VMEM)
-    smem = pl.BlockSpec(memory_space=pltpu.SMEM)
+    hbm = pl.BlockSpec(memory_space=pltpu.HBM)
     return pl.pallas_call(
         functools.partial(kernel, n_ctx, n_chan),
         out_shape=(
             jax.ShapeDtypeStruct((channels, local_len), F32),
             jax.ShapeDtypeStruct((channels, local_len), BF16),
         ),
-        in_specs=[vmem] * 5 + [smem] * 2,
+        in_specs=[hbm] * 7,
         out_specs=(vmem, vmem),
         scratch_shapes=[
+            pltpu.VMEM(rates.shape, F32),
+            pltpu.VMEM(residues.shape, F32),
+            pltpu.VMEM(value.shape, BF16),
+            pltpu.SMEM(skip.shape, F32),
+            pltpu.VMEM(residual.shape, F32),
+            pltpu.VMEM(gate.shape, BF16),
+            pltpu.SMEM(gain.shape, F32),
+            pltpu.SemaphoreType.DMA((7,)),
             pltpu.VMEM((channels, lanes), F32),
             pltpu.VMEM((n_ctx - 1, channels, lanes), F32),
             pltpu.VMEM((count, CHUNK), F32),
@@ -197,7 +225,10 @@
             bytes_accessed=14 * channels * local_len,
             transcendentals=64 * 1024,
         ),
-    )(value, gate, residual, rates, residues, skip, gain)
+    )(*[
+        pltpu.with_memory_space_constraint(x, pltpu.HBM)
+        for x in (value, gate, residual, rates, residues, skip, gain)
+    ])
 
 
 def solution(mesh):

time: 20.4 us -> 14.7 us (0.72)
  local copies, waits for them, and re-layouts: 6.54 us -> 1.29 us
  Pallas kernels: 12.9 us -> 12.6 us
    unnamed x16 -> x2, local copies, waits for them, and re-layouts: 6.54 us -> 1.29 us
    pallas_call x1, Pallas kernels: 12.9 us -> 12.6 us  [local(): pl.pallas_call(functools.partial(kernel, n_ctx, n_chan), out_shape=(jax.S...]
where the time goes in v1:
time: 14.7 us; the launch traced here: 14.5 us
  Pallas kernels  12.6 us (86%)
  local copies, waits for them, and re-layouts  1.29 us (9%)
  between operations  0.64 us (4%)
    pallas_call x1, Pallas kernels, local(): pl.pallas_call(functools.partial(kernel, n_ctx, n_chan), out_shape=(jax.S...  12.6 us
    unnamed x2, local copies, waits for them, and re-layouts  1.29 us

profile of v1, /device:TPU:0, one launch (start us, length us, event | category | flops | bytes accessed | tf_op | source)
XLA Modules:
  0.0 14.5 jit_solution(9294169950155980901)
XLA Ops:
  0.6 12.6 %shard_map.86 = (f32[8,4096]{1,0:T(8,128)S(1)}, bf16[8,4096]{1,0:T(8,128)(2,1)S(1)}) custom-call(bf16[8,4096]{1,0:T(8,128)(2,1)} %value_hbm.1, bf16[8,4096]{1,0:T(8,128)(2,1)} %gate_hbm.1, f32[8,4096]{1,0:T(8,128)} %residual_hbm.1, f32[8,16]{1,0:T(8,128)} %rates_hbm.1, f32[8,16]{1,0:T(8,128)} %residues_hbm.1, f32[8]{0:T(128)} %skip_hbm.1, f32[8]{0:T(128)} %gain_hbm.1), custom_call_target="tpu_custom_call" | custom-call | flops 184549376 | bytes 458752 | tf_op jit(solution)/shard_map/pallas_call | solution.py:194
  13.2 0.7 %copy.11 = f32[8,4096]{1,0:T(8,128)} copy(f32[8,4096]{1,0:T(8,128)S(1)} %get-tuple-element.4) | data formatting | bytes 262144
  13.9 0.6 %copy.12 = bf16[8,4096]{1,0:T(8,128)(2,1)} copy(bf16[8,4096]{1,0:T(8,128)(2,1)S(1)} %get-tuple-element.5) | data formatting | bytes 131072

commit v2 on v1

--- a/solution.py
+++ b/solution.py
@@ -35,7 +35,7 @@
     value_hbm, gate_hbm, residual_hbm, rates_hbm, residues_hbm, skip_hbm, gain_hbm,
     mixed_ref, normed_ref,
     rates_ref, residues_ref, value_ref, skip_ref, residual_ref, gate_ref, gain_ref, load_sem,
-    state_out, state_in, square_out, square_in,
+    carry_ref, state_out, state_in, square_out, square_in,
     state_send, state_recv, square_send, square_recv,
 ):
     loads = {}
@@ -59,9 +59,11 @@
 
     barrier = pltpu.get_barrier_semaphore()
     for step in range(1, n_ctx):
-        pl.semaphore_signal(
-            barrier, inc=1, device_id={"ctx": lax.rem(ctx + step, n_ctx)}, device_id_type=MESH
-        )
+        @pl.when(ctx >= step)
+        def _():
+            pl.semaphore_signal(
+                barrier, inc=1, device_id={"ctx": lax.rem(ctx - step + n_ctx, n_ctx)}, device_id_type=MESH
+            )
     for step in range(1, n_chan):
         pl.semaphore_signal(
             barrier, inc=1, device_id={"chan": lax.rem(chan + step, n_chan)}, device_id_type=MESH
@@ -106,7 +108,7 @@
         state = chunk_decay * state + chunk
     state_out[...] = state
 
-    pl.semaphore_wait(barrier, n_ctx - 1 + n_chan - 1)
+    pl.semaphore_wait(barrier, n_ctx - 1 - ctx + n_chan - 1)
     state_copies = []
     for step in range(1, n_ctx):
         copy = pltpu.make_async_remote_copy(
@@ -117,7 +119,7 @@
             device_id={"ctx": lax.rem(ctx + step, n_ctx)},
             device_id_type=MESH,
         )
-        copy.start()
+        pl.when(ctx + step < n_ctx)(copy.start)
         state_copies.append(copy)
 
     loads["skip"].wait()
@@ -145,11 +147,15 @@
     for name in ("residual", "gate", "gain"):
         loads[name].wait()
 
-    carry = jnp.zeros((channels, lanes), F32)
-    for step in range(1, n_ctx):
-        state_copies[step - 1].wait()
+    carry_ref[...] = jnp.zeros((channels, lanes), F32)
+    for step in range(1, n_ctx):
         decay = jnp.exp(-rate_lane * float(local_len * (step - 1)))
-        carry = carry + jnp.where(ctx >= step, decay, 0.0) * state_in[step - 1]
+
+        @pl.when(ctx >= step)
+        def _():
+            state_copies[step - 1].wait_recv()
+            carry_ref[...] += decay * state_in[step - 1]
+    carry = carry_ref[...]
     full = jnp.concatenate([states[k] + power[k:k + 1] * carry for k in range(count)], axis=0)
     far = lax.dot_general(
         jnp.concatenate(two_terms(full), axis=1), leave2, (((1,), (1,)), ((), ())),
@@ -179,6 +185,8 @@
     for step in range(1, n_chan):
         square_copies[step - 1].wait()
         total = total + square_in[step - 1]
+    for step in range(1, n_ctx):
+        pl.when(ctx + step < n_ctx)(state_copies[step - 1].wait_send)
     scale = lax.rsqrt(total / float(channels * n_chan) + 1e-06)
     for k in range(count):
         normed = mixed[k * channels:(k + 1) * channels] * scale[k:k + 1] * gain
@@ -209,6 +217,7 @@
             pltpu.SMEM(gain.shape, F32),
             pltpu.SemaphoreType.DMA((7,)),
             pltpu.VMEM((channels, lanes), F32),
+            pltpu.VMEM((channels, lanes), F32),
             pltpu.VMEM((n_ctx - 1, channels, lanes), F32),
             pltpu.VMEM((count, CHUNK), F32),
             pltpu.VMEM((n_chan - 1, count, CHUNK), F32),

time: 14.7 us -> 12.9 us (0.88)
  the two profiles are of different devices: /device:TPU:0 before, /device:TPU:9 now
where the time goes in v2:
time: 12.9 us; the launch traced here: 12.7 us
  Pallas kernels  10.8 us (84%)
  local copies, waits for them, and re-layouts  1.29 us (10%)
  between operations  0.64 us (5%)
    pallas_call x1, Pallas kernels, local(): pl.pallas_call(functools.partial(kernel, n_ctx, n_chan), out_shape=(jax.S...  10.8 us
    unnamed x2, local copies, waits for them, and re-layouts  1.29 us

profile of v2, /device:TPU:9, one launch (start us, length us, event | category | flops | bytes accessed | tf_op | source)
XLA Modules:
  0.0 12.7 jit_solution(8540455111983990198)
XLA Ops:
  0.6 10.8 %shard_map.86 = (f32[8,4096]{1,0:T(8,128)S(1)}, bf16[8,4096]{1,0:T(8,128)(2,1)S(1)}) custom-call(bf16[8,4096]{1,0:T(8,128)(2,1)} %value_hbm.1, bf16[8,4096]{1,0:T(8,128)(2,1)} %gate_hbm.1, f32[8,4096]{1,0:T(8,128)} %residual_hbm.1, f32[8,16]{1,0:T(8,128)} %rates_hbm.1, f32[8,16]{1,0:T(8,128)} %residues_hbm.1, f32[8]{0:T(128)} %skip_hbm.1, f32[8]{0:T(128)} %gain_hbm.1), custom_call_target="tpu_custom_call" | custom-call | flops 184549376 | bytes 458752 | tf_op jit(solution)/shard_map/pallas_call | solution.py:202
  11.4 0.7 %copy.11 = f32[8,4096]{1,0:T(8,128)} copy(f32[8,4096]{1,0:T(8,128)S(1)} %get-tuple-element.4) | data formatting | bytes 262144
  12.1 0.6 %copy.12 = bf16[8,4096]{1,0:T(8,128)(2,1)} copy(bf16[8,4096]{1,0:T(8,128)(2,1)S(1)} %get-tuple-element.5) | data formatting | bytes 131072

commit v3 on v2

--- a/solution.py
+++ b/solution.py
@@ -134,18 +134,28 @@
         toeplitz = jnp.where(target >= source, turned, 0.0)
         right.append(jnp.concatenate(two_terms(toeplitz), axis=1))
         left.append(jnp.where(channel_of == c, signal, 0.0).astype(BF16))
-    near = jnp.dot(
+    close = jnp.dot(
         jnp.concatenate(left, axis=1), jnp.concatenate(right, axis=0), preferred_element_type=F32
     )
     leave = weight_lane * jnp.exp(-rate_lane * (place + 1.0))
     leave2 = jnp.concatenate(two_terms(leave), axis=0)
     leave2 = jnp.concatenate([leave2, leave2], axis=1)
+    inside = lax.dot_general(
+        jnp.concatenate(two_terms(jnp.concatenate(states, axis=0)), axis=1), leave2,
+        (((1,), (1,)), ((), ())), preferred_element_type=F32,
+    )
+    near = close + inside
+    near = near[:, :CHUNK] + near[:, CHUNK:]
     power = jnp.exp(
         -rate_lane * (float(CHUNK) * lax.broadcasted_iota(jnp.int32, (count, lanes), 0).astype(F32))
     )
-
+    power = jnp.concatenate([jnp.where(own, power[k:k + 1], 0.0) for k in range(count)], axis=0)
+    power2 = jnp.concatenate(two_terms(power), axis=1)
     for name in ("residual", "gate", "gain"):
         loads[name].wait()
+    gate = stack_chunks(gate_ref[...].astype(F32), count)
+    base = stack_chunks(residual_ref[...], count) + gate * near
+    gain = column_of(gain_ref, channels)
 
     carry_ref[...] = jnp.zeros((channels, lanes), F32)
     for step in range(1, n_ctx):
@@ -155,15 +165,13 @@
         def _():
             state_copies[step - 1].wait_recv()
             carry_ref[...] += decay * state_in[step - 1]
-    carry = carry_ref[...]
-    full = jnp.concatenate([states[k] + power[k:k + 1] * carry for k in range(count)], axis=0)
+    carry = jnp.sum(carry_ref[...], axis=0, keepdims=True)
+    arrive2 = jnp.concatenate(two_terms(leave * carry), axis=0)
     far = lax.dot_general(
-        jnp.concatenate(two_terms(full), axis=1), leave2, (((1,), (1,)), ((), ())),
+        power2, jnp.concatenate([arrive2, arrive2], axis=1), (((1,), (1,)), ((), ())),
         preferred_element_type=F32,
     )
-    both = near + far
-    conv = both[:, :CHUNK] + both[:, CHUNK:]
-    mixed = stack_chunks(residual_ref[...], count) + stack_chunks(gate_ref[...].astype(F32), count) * conv
+    mixed = base + gate * (far[:, :CHUNK] + far[:, CHUNK:])
     square_out[...] = jnp.sum((mixed * mixed).reshape(count, channels, CHUNK), axis=1)
 
     square_copies = []
@@ -178,19 +186,22 @@
         )
         copy.start()
         square_copies.append(copy)
-    gain = column_of(gain_ref, channels)
+    gained = []
     for k in range(count):
-        mixed_ref[:, k * CHUNK:(k + 1) * CHUNK] = mixed[k * channels:(k + 1) * channels]
+        chunk = mixed[k * channels:(k + 1) * channels]
+        mixed_ref[:, k * CHUNK:(k + 1) * CHUNK] = chunk
+        gained.append(chunk * gain)
+    for step in range(1, n_ctx):
+        pl.when(ctx + step < n_ctx)(state_copies[step - 1].wait_send)
     total = square_out[...]
     for step in range(1, n_chan):
-        square_copies[step - 1].wait()
+        square_copies[step - 1].wait_recv()
         total = total + square_in[step - 1]
-    for step in range(1, n_ctx):
-        pl.when(ctx + step < n_ctx)(state_copies[step - 1].wait_send)
     scale = lax.rsqrt(total / float(channels * n_chan) + 1e-06)
     for k in range(count):
-        normed = mixed[k * channels:(k + 1) * channels] * scale[k:k + 1] * gain
-        normed_ref[:, k * CHUNK:(k + 1) * CHUNK] = normed.astype(BF16)
+        normed_ref[:, k * CHUNK:(k + 1) * CHUNK] = (gained[k] * scale[k:k + 1]).astype(BF16)
+    for step in range(1, n_chan):
+        square_copies[step - 1].wait_send()
 
 
 def local(n_ctx, n_chan, value, gate, residual, rates, residues, skip, gain):

time: 12.9 us -> 12.8 us (level)
  no operation moved by 1% of the time
where the time goes in v3:
time: 12.8 us; the launch traced here: 12.6 us
  Pallas kernels  10.7 us (84%)
  local copies, waits for them, and re-layouts  1.29 us (10%)
  between operations  0.64 us (5%)
    pallas_call x1, Pallas kernels, local(): pl.pallas_call(functools.partial(kernel, n_ctx, n_chan), out_shape=(jax.S...  10.7 us
    unnamed x2, local copies, waits for them, and re-layouts  1.29 us

profile of v3, /device:TPU:9, one launch (start us, length us, event | category | flops | bytes accessed | tf_op | source)
XLA Modules:
  0.0 12.6 jit_solution(841730592282404938)
XLA Ops:
  0.6 10.7 %shard_map.86 = (f32[8,4096]{1,0:T(8,128)S(1)}, bf16[8,4096]{1,0:T(8,128)(2,1)S(1)}) custom-call(bf16[8,4096]{1,0:T(8,128)(2,1)} %value_hbm.1, bf16[8,4096]{1,0:T(8,128)(2,1)} %gate_hbm.1, f32[8,4096]{1,0:T(8,128)} %residual_hbm.1, f32[8,16]{1,0:T(8,128)} %rates_hbm.1, f32[8,16]{1,0:T(8,128)} %residues_hbm.1, f32[8]{0:T(128)} %skip_hbm.1, f32[8]{0:T(128)} %gain_hbm.1), custom_call_target="tpu_custom_call" | custom-call | flops 184549376 | bytes 458752 | tf_op jit(solution)/shard_map/pallas_call | solution.py:213
  11.3 0.7 %copy.11 = f32[8,4096]{1,0:T(8,128)} copy(f32[8,4096]{1,0:T(8,128)S(1)} %get-tuple-element.4) | data formatting | bytes 262144
  12.0 0.6 %copy.12 = bf16[8,4096]{1,0:T(8,128)(2,1)} copy(bf16[8,4096]{1,0:T(8,128)(2,1)S(1)} %get-tuple-element.5) | data formatting | bytes 131072

commit v4 on v3

--- a/solution.py
+++ b/solution.py
@@ -33,7 +33,7 @@
 def kernel(
     n_ctx, n_chan,
     value_hbm, gate_hbm, residual_hbm, rates_hbm, residues_hbm, skip_hbm, gain_hbm,
-    mixed_ref, normed_ref,
+    base_out, added_out, scale_out,
     rates_ref, residues_ref, value_ref, skip_ref, residual_ref, gate_ref, gain_ref, load_sem,
     carry_ref, state_out, state_in, square_out, square_in,
     state_send, state_recv, square_send, square_recv,
@@ -171,7 +171,8 @@
         power2, jnp.concatenate([arrive2, arrive2], axis=1), (((1,), (1,)), ((), ())),
         preferred_element_type=F32,
     )
-    mixed = base + gate * (far[:, :CHUNK] + far[:, CHUNK:])
+    added = gate * (far[:, :CHUNK] + far[:, CHUNK:])
+    mixed = base + added
     square_out[...] = jnp.sum((mixed * mixed).reshape(count, channels, CHUNK), axis=1)
 
     square_copies = []
@@ -186,11 +187,10 @@
         )
         copy.start()
         square_copies.append(copy)
-    gained = []
     for k in range(count):
-        chunk = mixed[k * channels:(k + 1) * channels]
-        mixed_ref[:, k * CHUNK:(k + 1) * CHUNK] = chunk
-        gained.append(chunk * gain)
+        tokens = slice(k * CHUNK, (k + 1) * CHUNK)
+        base_out[:, tokens] = base[k * channels:(k + 1) * channels]
+        added_out[:, tokens] = added[k * channels:(k + 1) * channels]
     for step in range(1, n_ctx):
         pl.when(ctx + step < n_ctx)(state_copies[step - 1].wait_send)
     total = square_out[...]
@@ -199,7 +199,7 @@
         total = total + square_in[step - 1]
     scale = lax.rsqrt(total / float(channels * n_chan) + 1e-06)
     for k in range(count):
-        normed_ref[:, k * CHUNK:(k + 1) * CHUNK] = (gained[k] * scale[k:k + 1]).astype(BF16)
+        scale_out[:, k * CHUNK:(k + 1) * CHUNK] = gain * scale[k:k + 1]
     for step in range(1, n_chan):
         square_copies[step - 1].wait_send()
 
@@ -210,14 +210,15 @@
     count = local_len // CHUNK
     vmem = pl.BlockSpec(memory_space=pltpu.VMEM)
     hbm = pl.BlockSpec(memory_space=pltpu.HBM)
-    return pl.pallas_call(
+    base, added, scale = pl.pallas_call(
         functools.partial(kernel, n_ctx, n_chan),
         out_shape=(
             jax.ShapeDtypeStruct((channels, local_len), F32),
-            jax.ShapeDtypeStruct((channels, local_len), BF16),
+            jax.ShapeDtypeStruct((channels, local_len), F32),
+            jax.ShapeDtypeStruct((channels, local_len), F32),
         ),
         in_specs=[hbm] * 7,
-        out_specs=(vmem, vmem),
+        out_specs=(vmem, vmem, vmem),
         scratch_shapes=[
             pltpu.VMEM(rates.shape, F32),
             pltpu.VMEM(residues.shape, F32),
@@ -249,6 +250,8 @@
         pltpu.with_memory_space_constraint(x, pltpu.HBM)
         for x in (value, gate, residual, rates, residues, skip, gain)
     ])
+    mixed = base + added
+    return mixed, (mixed * scale).astype(BF16)
 
 
 def solution(mesh):

time: 12.8 us -> 12.2 us (0.953)
  local copies, waits for them, and re-layouts: 1.29 us -> 0 us
  other arithmetic: 0 us -> 0.69 us
    unnamed x2 -> x0, local copies, waits for them, and re-layouts: 1.29 us -> none
    convert_element_type x0 -> x1, other arithmetic: none -> 0.69 us  [local(): return (mixed, (mixed * scale).astype(BF16))]
where the time goes in v4:
time: 12.2 us; the launch traced here: 12 us
  Pallas kernels  10.7 us (88%)
  other arithmetic  0.69 us (6%)
  between operations  0.64 us (5%)
    pallas_call x1, Pallas kernels, local(): pl.pallas_call(functools.partial(kernel, n_ctx, n_chan), out_shape=(jax.S...  10.7 us
    convert_element_type x1, other arithmetic, local(): return (mixed, (mixed * scale).astype(BF16))  0.69 us

profile of v4, /device:TPU:9, one launch (start us, length us, event | category | flops | bytes accessed | tf_op | source)
XLA Modules:
  0.0 12.0 jit_solution(13223763291801093231)
XLA Ops:
  0.6 10.7 %shard_map.86 = (f32[8,4096]{1,0:T(8,128)S(1)}, f32[8,4096]{1,0:T(8,128)S(1)}, f32[8,4096]{1,0:T(8,128)S(1)}) custom-call(bf16[8,4096]{1,0:T(8,128)(2,1)} %value_hbm.1, bf16[8,4096]{1,0:T(8,128)(2,1)} %gate_hbm.1, f32[8,4096]{1,0:T(8,128)} %residual_hbm.1, f32[8,16]{1,0:T(8,128)} %rates_hbm.1, f32[8,16]{1,0:T(8,128)} %residues_hbm.1, f32[8]{0:T(128)} %skip_hbm.1, ...), custom_call_target="tpu_custom_call" | custom-call | flops 184549376 | bytes 458752 | tf_op jit(solution)/shard_map/pallas_call | solution.py:213
  11.3 0.7 %multiply_convert_fusion = (bf16[8,4096]{1,0:T(8,128)(2,1)}, f32[8,4096]{1,0:T(8,128)}) fusion(f32[8,4096]{1,0:T(8,128)S(1)} %get-tuple-element.7, f32[8,4096]{1,0:T(8,128)S(1)} %get-tuple-element.5, f32[8,4096]{1,0:T(8,128)S(1)} %get-tuple-element.6), kind=kLoop, calls=%fused_computation | loop fusion | flops 98304 | bytes 589824 | tf_op jit(solution)/shard_map/convert_element_type | solution.py:254

commit v5 on v4

--- a/solution.py
+++ b/solution.py
@@ -38,6 +38,25 @@
     carry_ref, state_out, state_in, square_out, square_in,
     state_send, state_recv, square_send, square_recv,
 ):
+    ctx = lax.axis_index("ctx")
+    chan = lax.axis_index("chan")
+    channels, local_len = value_ref.shape
+    modes = rates_ref.shape[1]
+    lanes = channels * modes
+    count = local_len // CHUNK
+
+    barrier = pltpu.get_barrier_semaphore()
+    for step in range(n_ctx - 1, 0, -1):
+        @pl.when(ctx >= step)
+        def _():
+            pl.semaphore_signal(
+                barrier, inc=1, device_id={"ctx": lax.rem(ctx - step + n_ctx, n_ctx)}, device_id_type=MESH
+            )
+    for step in range(1, n_chan):
+        pl.semaphore_signal(
+            barrier, inc=1, device_id={"chan": lax.rem(chan + step, n_chan)}, device_id_type=MESH
+        )
+
     loads = {}
     for order, (name, source, target) in enumerate([
         ("rates", rates_hbm, rates_ref),
@@ -50,24 +69,6 @@
     ]):
         loads[name] = pltpu.make_async_copy(source, target, load_sem.at[order])
         loads[name].start()
-    ctx = lax.axis_index("ctx")
-    chan = lax.axis_index("chan")
-    channels, local_len = value_ref.shape
-    modes = rates_ref.shape[1]
-    lanes = channels * modes
-    count = local_len // CHUNK
-
-    barrier = pltpu.get_barrier_semaphore()
-    for step in range(1, n_ctx):
-        @pl.when(ctx >= step)
-        def _():
-            pl.semaphore_signal(
-                barrier, inc=1, device_id={"ctx": lax.rem(ctx - step + n_ctx, n_ctx)}, device_id_type=MESH
-            )
-    for step in range(1, n_chan):
-        pl.semaphore_signal(
-            barrier, inc=1, device_id={"chan": lax.rem(chan + step, n_chan)}, device_id_type=MESH
-        )
 
     loads["rates"].wait()
     loads["residues"].wait()
@@ -106,21 +107,7 @@
         states.append(state)
         chunk = jnp.where(own, added[k * channels:(k + 1) * channels], 0.0)
         state = chunk_decay * state + chunk
-    state_out[...] = state
-
-    pl.semaphore_wait(barrier, n_ctx - 1 - ctx + n_chan - 1)
-    state_copies = []
-    for step in range(1, n_ctx):
-        copy = pltpu.make_async_remote_copy(
-            src_ref=state_out,
-            dst_ref=state_in.at[step - 1],
-            send_sem=state_send.at[step - 1],
-            recv_sem=state_recv.at[step - 1],
-            device_id={"ctx": lax.rem(ctx + step, n_ctx)},
-            device_id_type=MESH,
-        )
-        pl.when(ctx + step < n_ctx)(copy.start)
-        state_copies.append(copy)
+    state_out[...] = jnp.sum(state, axis=0, keepdims=True)
 
     loads["skip"].wait()
     taps = taps + jnp.where(token == 0, column_of(skip_ref, channels), 0.0)
@@ -151,21 +138,34 @@
     )
     power = jnp.concatenate([jnp.where(own, power[k:k + 1], 0.0) for k in range(count)], axis=0)
     power2 = jnp.concatenate(two_terms(power), axis=1)
+    decays = [jnp.exp(-rate_lane * float(local_len * step)) for step in range(n_ctx - 1)]
     for name in ("residual", "gate", "gain"):
         loads[name].wait()
     gate = stack_chunks(gate_ref[...].astype(F32), count)
     base = stack_chunks(residual_ref[...], count) + gate * near
     gain = column_of(gain_ref, channels)
 
-    carry_ref[...] = jnp.zeros((channels, lanes), F32)
+    pl.semaphore_wait(barrier, n_ctx - 1 - ctx + n_chan - 1)
+    state_copies = {}
+    for step in range(n_ctx - 1, 0, -1):
+        copy = pltpu.make_async_remote_copy(
+            src_ref=state_out,
+            dst_ref=state_in.at[step - 1],
+            send_sem=state_send.at[step - 1],
+            recv_sem=state_recv.at[step - 1],
+            device_id={"ctx": lax.rem(ctx + step, n_ctx)},
+            device_id_type=MESH,
+        )
+        pl.when(ctx + step < n_ctx)(copy.start)
+        state_copies[step] = copy
+
+    carry_ref[...] = jnp.zeros((1, lanes), F32)
     for step in range(1, n_ctx):
-        decay = jnp.exp(-rate_lane * float(local_len * (step - 1)))
-
         @pl.when(ctx >= step)
         def _():
-            state_copies[step - 1].wait_recv()
-            carry_ref[...] += decay * state_in[step - 1]
-    carry = jnp.sum(carry_ref[...], axis=0, keepdims=True)
+            state_copies[step].wait_recv()
+            carry_ref[...] += decays[step - 1] * state_in[step - 1]
+    carry = carry_ref[...]
     arrive2 = jnp.concatenate(two_terms(leave * carry), axis=0)
     far = lax.dot_general(
         power2, jnp.concatenate([arrive2, arrive2], axis=1), (((1,), (1,)), ((), ())),
@@ -192,7 +192,7 @@
         base_out[:, tokens] = base[k * channels:(k + 1) * channels]
         added_out[:, tokens] = added[k * channels:(k + 1) * channels]
     for step in range(1, n_ctx):
-        pl.when(ctx + step < n_ctx)(state_copies[step - 1].wait_send)
+        pl.when(ctx + step < n_ctx)(state_copies[step].wait_send)
     total = square_out[...]
     for step in range(1, n_chan):
         square_copies[step - 1].wait_recv()
@@ -228,9 +228,9 @@
             pltpu.VMEM(gate.shape, BF16),
             pltpu.SMEM(gain.shape, F32),
             pltpu.SemaphoreType.DMA((7,)),
-            pltpu.VMEM((channels, lanes), F32),
-            pltpu.VMEM((channels, lanes), F32),
-            pltpu.VMEM((n_ctx - 1, channels, lanes), F32),
+            pltpu.VMEM((1, lanes), F32),
+            pltpu.VMEM((1, lanes), F32),
+            pltpu.VMEM((n_ctx - 1, 1, lanes), F32),
             pltpu.VMEM((count, CHUNK), F32),
             pltpu.VMEM((n_chan - 1, count, CHUNK), F32),
             pltpu.SemaphoreType.DMA((n_ctx - 1,)),

time: 12.2 us -> 12.1 us (level)
  no operation moved by 1% of the time
where the time goes in v5:
time: 12.1 us; the launch traced here: 11.9 us
  Pallas kernels  10.6 us (88%)
  other arithmetic  0.69 us (6%)
  between operations  0.64 us (5%)
    pallas_call x1, Pallas kernels, local(): pl.pallas_call(functools.partial(kernel, n_ctx, n_chan), out_shape=(jax.S...  10.6 us
    convert_element_type x1, other arithmetic, local(): return (mixed, (mixed * scale).astype(BF16))  0.69 us

profile of v5, /device:TPU:9, one launch (start us, length us, event | category | flops | bytes accessed | tf_op | source)
XLA Modules:
  0.0 11.9 jit_solution(17027975842333307266)
XLA Ops:
  0.6 10.6 %shard_map.86 = (f32[8,4096]{1,0:T(8,128)S(1)}, f32[8,4096]{1,0:T(8,128)S(1)}, f32[8,4096]{1,0:T(8,128)S(1)}) custom-call(bf16[8,4096]{1,0:T(8,128)(2,1)} %value_hbm.1, bf16[8,4096]{1,0:T(8,128)(2,1)} %gate_hbm.1, f32[8,4096]{1,0:T(8,128)} %residual_hbm.1, f32[8,16]{1,0:T(8,128)} %rates_hbm.1, f32[8,16]{1,0:T(8,128)} %residues_hbm.1, f32[8]{0:T(128)} %skip_hbm.1, ...), custom_call_target="tpu_custom_call" | custom-call | flops 184549376 | bytes 458752 | tf_op jit(solution)/shard_map/pallas_call | solution.py:213
  11.2 0.7 %multiply_convert_fusion = (bf16[8,4096]{1,0:T(8,128)(2,1)}, f32[8,4096]{1,0:T(8,128)}) fusion(f32[8,4096]{1,0:T(8,128)S(1)} %get-tuple-element.7, f32[8,4096]{1,0:T(8,128)S(1)} %get-tuple-element.5, f32[8,4096]{1,0:T(8,128)S(1)} %get-tuple-element.6), kind=kLoop, calls=%fused_computation | loop fusion | flops 98304 | bytes 589824 | tf_op jit(solution)/shard_map/convert_element_type | solution.py:254

commit v6 on v5

--- a/solution.py
+++ b/solution.py
@@ -175,8 +175,9 @@
     mixed = base + added
     square_out[...] = jnp.sum((mixed * mixed).reshape(count, channels, CHUNK), axis=1)
 
-    square_copies = []
-    for step in range(1, n_chan):
+    square_copies = {}
+    order = sorted(range(1, n_chan), key=lambda step: -min(step, n_chan - step))
+    for step in order:
         copy = pltpu.make_async_remote_copy(
             src_ref=square_out,
             dst_ref=square_in.at[step - 1],
@@ -186,7 +187,7 @@
             device_id_type=MESH,
         )
         copy.start()
-        square_copies.append(copy)
+        square_copies[step] = copy
     for k in range(count):
         tokens = slice(k * CHUNK, (k + 1) * CHUNK)
         base_out[:, tokens] = base[k * channels:(k + 1) * channels]
@@ -195,13 +196,13 @@
         pl.when(ctx + step < n_ctx)(state_copies[step].wait_send)
     total = square_out[...]
     for step in range(1, n_chan):
-        square_copies[step - 1].wait_recv()
+        square_copies[step].wait_recv()
         total = total + square_in[step - 1]
     scale = lax.rsqrt(total / float(channels * n_chan) + 1e-06)
     for k in range(count):
         scale_out[:, k * CHUNK:(k + 1) * CHUNK] = gain * scale[k:k + 1]
     for step in range(1, n_chan):
-        square_copies[step - 1].wait_send()
+        square_copies[step].wait_send()
 
 
 def local(n_ctx, n_chan, value, gate, residual, rates, residues, skip, gain):

time: 12.1 us -> 12 us (level)
  the two profiles are of different devices: /device:TPU:9 before, /device:TPU:8 now
where the time goes in v6:
time: 12 us; the launch traced here: 11.8 us
  Pallas kernels  10.5 us (88%)
  other arithmetic  0.69 us (6%)
  between operations  0.64 us (5%)
    pallas_call x1, Pallas kernels, local(): pl.pallas_call(functools.partial(kernel, n_ctx, n_chan), out_shape=(jax.S...  10.5 us
    convert_element_type x1, other arithmetic, local(): return (mixed, (mixed * scale).astype(BF16))  0.69 us

profile of v6, /device:TPU:8, one launch (start us, length us, event | category | flops | bytes accessed | tf_op | source)
XLA Modules:
  0.0 11.8 jit_solution(689301441702403786)
XLA Ops:
  0.6 10.5 %shard_map.86 = (f32[8,4096]{1,0:T(8,128)S(1)}, f32[8,4096]{1,0:T(8,128)S(1)}, f32[8,4096]{1,0:T(8,128)S(1)}) custom-call(bf16[8,4096]{1,0:T(8,128)(2,1)} %value_hbm.1, bf16[8,4096]{1,0:T(8,128)(2,1)} %gate_hbm.1, f32[8,4096]{1,0:T(8,128)} %residual_hbm.1, f32[8,16]{1,0:T(8,128)} %rates_hbm.1, f32[8,16]{1,0:T(8,128)} %residues_hbm.1, f32[8]{0:T(128)} %skip_hbm.1, ...), custom_call_target="tpu_custom_call" | custom-call | flops 184549376 | bytes 458752 | tf_op jit(solution)/shard_map/pallas_call | solution.py:214
  11.1 0.7 %multiply_convert_fusion = (bf16[8,4096]{1,0:T(8,128)(2,1)}, f32[8,4096]{1,0:T(8,128)}) fusion(f32[8,4096]{1,0:T(8,128)S(1)} %get-tuple-element.7, f32[8,4096]{1,0:T(8,128)S(1)} %get-tuple-element.5, f32[8,4096]{1,0:T(8,128)S(1)} %get-tuple-element.6), kind=kLoop, calls=%fused_computation | loop fusion | flops 98304 | bytes 589824 | tf_op jit(solution)/shard_map/convert_element_type | solution.py:255

commit v7 on v6

--- a/solution.py
+++ b/solution.py
@@ -137,7 +137,8 @@
         -rate_lane * (float(CHUNK) * lax.broadcasted_iota(jnp.int32, (count, lanes), 0).astype(F32))
     )
     power = jnp.concatenate([jnp.where(own, power[k:k + 1], 0.0) for k in range(count)], axis=0)
-    power2 = jnp.concatenate(two_terms(power), axis=1)
+    turned2 = jnp.concatenate(two_terms(leave.T), axis=1)
+    turned2 = jnp.concatenate([turned2, turned2], axis=0)
     decays = [jnp.exp(-rate_lane * float(local_len * step)) for step in range(n_ctx - 1)]
     for name in ("residual", "gate", "gain"):
         loads[name].wait()
@@ -166,11 +167,8 @@
             state_copies[step].wait_recv()
             carry_ref[...] += decays[step - 1] * state_in[step - 1]
     carry = carry_ref[...]
-    arrive2 = jnp.concatenate(two_terms(leave * carry), axis=0)
-    far = lax.dot_general(
-        power2, jnp.concatenate([arrive2, arrive2], axis=1), (((1,), (1,)), ((), ())),
-        preferred_element_type=F32,
-    )
+    arrive2 = jnp.concatenate(two_terms(power * carry), axis=1)
+    far = jnp.dot(arrive2, turned2, preferred_element_type=F32)
     added = gate * (far[:, :CHUNK] + far[:, CHUNK:])
     mixed = base + added
     square_out[...] = jnp.sum((mixed * mixed).reshape(count, channels, CHUNK), axis=1)

time: 12 us -> 12 us (level)
  no operation moved by 1% of the time
where the time goes in v7:
time: 12 us; the launch traced here: 11.8 us
  Pallas kernels  10.4 us (87%)
  other arithmetic  0.69 us (6%)
  between operations  0.64 us (5%)
    pallas_call x1, Pallas kernels, local(): pl.pallas_call(functools.partial(kernel, n_ctx, n_chan), out_shape=(jax.S...  10.4 us
    convert_element_type x1, other arithmetic, local(): return (mixed, (mixed * scale).astype(BF16))  0.69 us

profile of v7, /device:TPU:8, one launch (start us, length us, event | category | flops | bytes accessed | tf_op | source)
XLA Modules:
  0.0 11.8 jit_solution(10762327253921160991)
XLA Ops:
  0.6 10.4 %shard_map.86 = (f32[8,4096]{1,0:T(8,128)S(1)}, f32[8,4096]{1,0:T(8,128)S(1)}, f32[8,4096]{1,0:T(8,128)S(1)}) custom-call(bf16[8,4096]{1,0:T(8,128)(2,1)} %value_hbm.1, bf16[8,4096]{1,0:T(8,128)(2,1)} %gate_hbm.1, f32[8,4096]{1,0:T(8,128)} %residual_hbm.1, f32[8,16]{1,0:T(8,128)} %rates_hbm.1, f32[8,16]{1,0:T(8,128)} %residues_hbm.1, f32[8]{0:T(128)} %skip_hbm.1, ...), custom_call_target="tpu_custom_call" | custom-call | flops 184549376 | bytes 458752 | tf_op jit(solution)/shard_map/pallas_call | solution.py:212
  11.1 0.7 %multiply_convert_fusion = (bf16[8,4096]{1,0:T(8,128)(2,1)}, f32[8,4096]{1,0:T(8,128)}) fusion(f32[8,4096]{1,0:T(8,128)S(1)} %get-tuple-element.7, f32[8,4096]{1,0:T(8,128)S(1)} %get-tuple-element.5, f32[8,4096]{1,0:T(8,128)S(1)} %get-tuple-element.6), kind=kLoop, calls=%fused_computation | loop fusion | flops 98304 | bytes 589824 | tf_op jit(solution)/shard_map/convert_element_type | solution.py:253
